TPU v7x, 128 devices: a whole 4x4x4 slice. The times are simulated.
128 devices in a mesh: pipe: 4 (over y), seq: 32 (over z, x, core).
Axes of the slice: x: 4, y: 4, z: 4, core: 2. Of those that a mesh axis runs over, the one named last changes fastest.
Arguments:
- hidden_in: bfloat16 [3072, 1536], P('seq'), may hold values from -6 to 6
- modulation: float32 [4, 3, 1536], P('pipe'), may hold values from -3 to 3
- w_qkv: bfloat16 [4, 1536, 4608], P('pipe'), may hold values from -0.15625 to 0.15625
- w_out: bfloat16 [4, 1536, 1536], P('pipe'), may hold values from -0.15625 to 0.15625
- qk_gain: float32 [4, 2, 128], P('pipe'), may hold values from 1.2 to 2.4
- stale_kv: bfloat16 [4, 3072, 2, 1536], P('pipe', 'seq'), may hold values from -6 to 6
- positions: int32 [3072, 3], P('seq'), may hold values from 0 to 63, as said below
- order: int32 [4], replicated, may hold values from 0 to 3, each once
Outputs:
- hidden_out: bfloat16 [4, 3072, 1536], P('pipe', 'seq')
- fresh_kv: bfloat16 [4, 3072, 2, 1536], P('pipe', 'seq')
Inputs may be any that keep to these rules, and one draw needn't show every extreme that they name: `positions`: distinct tokens have distinct (row, column); the text index is below 4, the row below 48 and the column below 64. `order`: each patch number once.
All inputs are finite; a program needn't handle non-finite values.
Results may differ from a plain program's by a relative error of at most 0.04.
Values may be sent and summed in bfloat16 or wider, within the bound.
No kernel may reach another device: no remote copies, remote signals or barrier semaphores. Data moves between devices by JAX's collectives and lax.ppermute only.
A program may use at most 64 MiB of HBM per device.

v0:
```python
import functools
import math

import jax
import jax.numpy as jnp
from jax import lax
from jax.experimental import pallas as pl
from jax.experimental.pallas import tpu as pltpu
from jax.sharding import Mesh
from jax.sharding import PartitionSpec as P

GROUPS = 2
PATCHES = 4
HEAD = 128
HEADS = 12
CHIPS = 16
PD = 24
D = 1536
LAYERS = 4
PER = PATCHES // GROUPS
N = PER * PD
QUERIES = CHIPS * PD
KEYS = 2 * CHIPS * PD
ROWS = PER * 3 * PD
WIDE = 4 * HEAD
F32 = jnp.float32
BF16 = jnp.bfloat16


def rotary_tables(positions):
    lane = lax.broadcasted_iota(jnp.int32, (8, HEAD), 1)
    row = lax.broadcasted_iota(jnp.int32, (8, HEAD), 0)
    pair = lane >> 1
    axis = jnp.where(pair < 8, 0, jnp.where(pair < 36, 1, 2))
    start = jnp.where(pair < 8, 0, jnp.where(pair < 36, 8, 36))
    width = jnp.where(pair < 8, 16.0, 56.0)
    freq = jnp.exp((pair - start).astype(F32) / width * (-2.0 * math.log(10000.0)))[0:1]
    even = jnp.where((lane & 1) == 0, 1.0, 0.0)[0:1]
    picks = jnp.where(axis == row, 1.0, 0.0)[0:3].astype(BF16)
    angle = freq * lax.dot_general(
        positions.astype(F32).astype(BF16),
        picks,
        (((0,), (0,)), ((), ())),
        preferred_element_type=F32,
    )
    cos, sin = jnp.cos(angle), jnp.sin(angle)
    return jnp.concatenate([cos, -sin * even, sin * (1.0 - even)], axis=1)


def hats(x, gain, tab, by_dot=False):
    if by_dot:
        ones = jnp.ones((HEAD, HEAD), BF16)
        square = x * x
        high = square.astype(BF16)
        low = (square - high.astype(F32)).astype(BF16)
        square = sum(jnp.dot(t, ones, preferred_element_type=F32) for t in (high, low)) / HEAD
    else:
        square = jnp.mean(x * x, axis=-1, keepdims=True)
    inv = lax.rsqrt(square + 1e-6)
    x = x * inv * gain
    return (
        x * tab[:, :HEAD]
        + pltpu.roll(x, HEAD - 1, 1) * tab[:, HEAD : 2 * HEAD]
        + pltpu.roll(x, 1, 1) * tab[:, 2 * HEAD :]
    )


def stage(info_ref, turn):
    section = info_ref[0]
    g = jnp.clip(turn - section, 0, GROUPS - 1)
    ids = [info_ref[1 + g * PER + j] for j in range(PER)]
    return section, g, ids


def rows_of(info_ref, turn, x_ref, recv_ref):
    section, _, ids = stage(info_ref, turn)
    own = jnp.concatenate([x_ref[p].astype(F32) for p in ids], axis=0)
    if recv_ref is None:
        return own
    sent = jnp.concatenate([recv_ref[j].astype(F32) for j in range(PER)], axis=0)
    return jnp.where(section == 0, own, sent)


def lanes_from(start):
    if isinstance(start, int):
        return slice(start, start + WIDE)
    return pl.ds(pl.multiple_of(start, WIDE), WIDE)


def project_kernel(turn, last, *refs):
    first = turn == 0
    refs = list(refs)
    info_ref, x_ref = refs[:2]
    refs = refs[2:]
    recv_ref = None if first else refs.pop(0)
    mod_ref, w_ref, gain_ref = refs[:3]
    refs = refs[3:]
    q_gain = gain_ref[0, 0:1, :] * (math.log2(math.e) / math.sqrt(HEAD))
    k_gain = gain_ref[0, 1:2, :]
    if first:
        pos_ref, stale_ref, chunk_ref, fresh_ref, tab_ref, held_ref, sems = refs
        copies = []
        for block in range(D // WIDE):
            for part in range(3):
                cols = pl.ds(part * D + block * WIDE, WIDE)
                copies.append(
                    pltpu.make_async_copy(
                        w_ref.at[0, :, cols], held_ref.at[:, cols], sems.at[len(copies)]
                    )
                )
        for copy in copies[:6]:
            copy.start()
        tab_ref[...] = rotary_tables(pos_ref[...]).reshape(PATCHES, PD, 3 * HEAD)
        tabs = jnp.concatenate([tab_ref[info_ref[1 + r]] for r in range(1, PATCHES)], axis=0)

        def stale_block(block):
            ready = []
            for h in range(block * (WIDE // HEAD), (block + 1) * (WIDE // HEAD)):
                parts = []
                for r in range(1, PATCHES):
                    p = info_ref[1 + r]
                    ks = stale_ref[p, :, h * HEAD : (h + 1) * HEAD].astype(F32)
                    vs = stale_ref[p, :, D + h * HEAD : D + (h + 1) * HEAD].astype(F32)
                    parts += [ks, vs]
                ready.append((h, parts))
            for i, (h, parts) in enumerate(ready):
                ks = jnp.concatenate(parts[0::2], axis=0)
                ks = hats(ks, k_gain, tabs, by_dot=True)
                for r in range(3):
                    parts[2 * r] = ks[PD * r : PD * (r + 1)]
                ready[i] = (h, jnp.concatenate(parts, axis=0).astype(BF16))
            for h, rows in ready:
                chunk_ref[h, ROWS:] = rows

    else:
        tab_ref, chunk_ref, fresh_ref = refs
    _, _, ids = stage(info_ref, turn)
    rows = rows_of(info_ref, turn, x_ref, recv_ref)
    centred = rows - jnp.mean(rows, axis=-1, keepdims=True)
    spread = jnp.mean(centred * centred, axis=-1, keepdims=True)
    modulated = (
        centred * lax.rsqrt(spread + 1e-6) * (1.0 + mod_ref[1]) + mod_ref[0]
    ).astype(BF16)
    tab = jnp.concatenate([tab_ref[p] for p in ids], axis=0)
    for c in range(HEADS, CHIPS):
        chunk_ref[c] = jnp.zeros(chunk_ref.shape[1:], BF16)
    def step(block, carry):
        if first and block == 0:
            stale_block(0)
            for copy in copies[6:]:
                copy.start()
        done = []
        for part in range(3):
            cols = lanes_from(part * D + block * WIDE)
            if first:
                copies[3 * block + part].wait()
                w = held_ref[:, cols]
            else:
                w = w_ref[0, :, cols]
            done.append(jnp.dot(modulated, w, preferred_element_type=F32))
        if first and block + 1 < D // WIDE:
            stale_block(block + 1)
        q, k, v = done
        k16, v16 = k.astype(BF16), v.astype(BF16)
        k, v = k16.astype(F32), v16.astype(F32)
        here = lanes_from(block * WIDE)
        if last:
            for j in range(PER):
                both = [t[PD * j : PD * (j + 1)] for t in (k, v)]
                fresh_ref[j, :, :, here] = jnp.stack(both, axis=1).astype(BF16)
        else:
            fresh_ref[:, here] = k16
            fresh_ref[:, lanes_from(D + block * WIDE)] = v16
        for i in range(WIDE // HEAD):
            h = block * (WIDE // HEAD) + i
            lanes = slice(i * HEAD, (i + 1) * HEAD)
            qh = hats(q[:, lanes], q_gain, tab)
            kh = hats(k[:, lanes], k_gain, tab)
            vh = v[:, lanes]
            parts = []
            for j in range(PER):
                here = slice(PD * j, PD * (j + 1))
                parts += [qh[here], kh[here], vh[here]]
            chunk_ref[h, :ROWS] = jnp.concatenate(parts, axis=0).astype(BF16)
        return carry

    if first:
        for block in range(D // WIDE):
            step(block, 0)
    else:
        lax.fori_loop(0, D // WIDE, step, 0)


def taken(ref, start):
    rows = ref[...].astype(F32)[:, start : start + PD, :]
    return rows.reshape(CHIPS * PD, HEAD).astype(BF16)


def weighed(q, k, v):
    s = lax.dot_general(q, k, (((1,), (1,)), ((), ())), preferred_element_type=F32)
    w = jnp.exp2(s).astype(BF16)
    v = jnp.concatenate([v, jnp.ones(v.shape, BF16)], axis=1)
    return jnp.dot(w, v, preferred_element_type=F32)


def half(ref, q):
    k = [taken(ref, 3 * PD * j + PD) for j in range(PER)]
    v = [taken(ref, 3 * PD * j + 2 * PD) for j in range(PER)]
    return weighed(q, k[0], v[0]), weighed(q[QUERIES:], k[1], v[1])


def half_stale(ref, q):
    keys = [taken(ref, ROWS + 2 * PD * n) for n in range(3)]
    values = [taken(ref, ROWS + 2 * PD * n + PD) for n in range(3)]
    return sum(weighed(q, keys[n], values[n]) for n in (1, 2)), weighed(
        q[:QUERIES], keys[0], values[0]
    )


def both_queries(own_ref):
    return jnp.concatenate([taken(own_ref, 3 * PD * j) for j in range(PER)], axis=0)


def early_kernel(turn, info_ref, own_ref, *refs):
    first = turn == 0
    sum_ref = refs[-1]
    q = both_queries(own_ref)
    total, second = half(own_ref, q)
    if first:
        more, lead = half_stale(own_ref, q)
        total = total + more
    else:
        k_ref, v_ref = refs[:2]
        _, g, _ = stage(info_ref, turn)
        base = g * PER
        lead = weighed(q[:QUERIES], k_ref[base + 1], v_ref[base + 1])
        for n in range(PATCHES - PER):
            slot = jnp.where(n < base, n, n + PER)
            total = total + weighed(q, k_ref[slot], v_ref[slot])
    sum_ref[:QUERIES] = total[:QUERIES] + lead
    sum_ref[QUERIES:] = total[QUERIES:] + second


def late_kernel(turn, own_ref, oth_ref, sum_ref, out_ref):
    q = both_queries(own_ref)
    total, second = half(oth_ref, q)
    total = total + sum_ref[...]
    lead, second = total[:QUERIES], total[QUERIES:] + second
    if turn == 0:
        more, extra = half_stale(oth_ref, q)
        lead = lead + more[:QUERIES] + extra
        second = second + more[QUERIES:]
    outs = [
        (t[:, :HEAD] / t[:, HEAD:]).reshape(CHIPS, PD, HEAD) for t in (lead, second)
    ]
    out_ref[...] = jnp.concatenate(outs, axis=1).astype(BF16)


def keep_kernel(turn, info_ref, raw_ref, own_ref, oth_ref, *refs):
    section, g, _ = stage(info_ref, turn)
    kout_ref, vout_ref, pair_ref = refs[-3:]
    paired(raw_ref, pair_ref)
    pairs = ((own_ref, 0), (oth_ref, CHIPS * PD))

    def put(slot, start, old_ref, new_ref, keep):
        for ref, row in pairs:
            fresh = taken(ref, start)
            if old_ref is not None:
                old = old_ref[slot, row : row + CHIPS * PD]
                fresh = jnp.where(keep, fresh, old)
            new_ref[slot, row : row + CHIPS * PD] = fresh

    if turn == 0:
        put(0, PD, None, kout_ref, None)
        put(0, 2 * PD, None, vout_ref, None)
        for r in range(1, PATCHES):
            put(r, ROWS + 2 * PD * (r - 1), None, kout_ref, None)
            put(r, ROWS + 2 * PD * (r - 1) + PD, None, vout_ref, None)
        for j in range(1, PER):
            put(j, 3 * PD * j + PD, kout_ref, kout_ref, section == 0)
            put(j, 3 * PD * j + 2 * PD, vout_ref, vout_ref, section == 0)
        return
    kin_ref, vin_ref = refs[:2]
    base = g * PER
    begun = turn >= section
    for n in range(PATCHES - PER):
        slot = jnp.where(n < base, n, n + PER)
        kout_ref[slot] = kin_ref[slot]
        vout_ref[slot] = vin_ref[slot]
    for j in range(PER):
        put(base + j, 3 * PD * j + PD, kin_ref, kout_ref, begun)
        put(base + j, 3 * PD * j + 2 * PD, vin_ref, vout_ref, begun)


def paired(ref, out_ref):
    for j in range(PER):
        for c in range(0, D, WIDE):
            k, v = (
                ref[:, at : at + WIDE].astype(F32)[PD * j : PD * (j + 1)] for at in (c, D + c)
            )
            out_ref[j, :, :, c : c + WIDE] = jnp.stack([k, v], axis=1).astype(BF16)


def place(info_ref, section, olds, out_ref, sems, skip=None):
    copies = []
    for g in range(GROUPS):
        if section + g == skip:
            continue
        for j in range(PER):
            r = g * PER + j
            copies.append(
                pltpu.make_async_copy(
                    olds[section + g].at[j], out_ref.at[info_ref[1 + r]], sems.at[r]
                )
            )
            copies[-1].start()
    return copies


def output_kernel(turn, last, *refs):
    first = turn == 0
    refs = list(refs)
    info_ref, att_ref, w_ref, x_ref = refs[:4]
    refs = refs[4:]
    recv_ref = None if first else refs.pop(0)
    mod_ref = refs.pop(0)

    def store(ref):
        att = jnp.concatenate([att_ref[h] for h in range(HEADS)], axis=1)
        rows = rows_of(info_ref, turn, x_ref, recv_ref)
        branch = jnp.dot(att, w_ref[0], preferred_element_type=F32)
        new = rows + mod_ref[2] * branch
        for j in range(PER):
            ref[j] = new[PD * j : PD * (j + 1)].astype(BF16)

    if not last:
        store(refs[0])
        return
    *refs, out_ref, kept_ref, new_ref, sems, kept_sems = refs
    fresh = refs[: turn + 1]
    olds = refs[turn + 1 :] + [new_ref]
    for section in range(LAYERS):

        @pl.when(info_ref[0] == section)
        def _():
            copies = place(info_ref, section, fresh, kept_ref, kept_sems)
            copies += place(info_ref, section, olds, out_ref, sems, turn)
            if section == LAYERS - 1:
                store(new_ref)
                copies += place(info_ref, section, olds, out_ref, sems, turn - 1)
            for copy in copies:
                copy.wait()


SMEM = pl.BlockSpec(memory_space=pltpu.SMEM)
VMEM = pl.BlockSpec(memory_space=pltpu.VMEM)
HBM = pl.BlockSpec(memory_space=pltpu.HBM)


def shape(*dims, dtype=BF16):
    return jax.ShapeDtypeStruct(dims, dtype)


def call(
    kernel, name, out_shape, args, limit=20, specs=None, scratch=(), flops=10**9, outs=None
):
    return pl.pallas_call(
        kernel,
        out_shape=out_shape,
        in_specs=specs or [SMEM] + [VMEM] * (len(args) - 1),
        out_specs=[outs or VMEM] * len(out_shape),
        scratch_shapes=list(scratch),
        compiler_params=pltpu.CompilerParams(vmem_limit_bytes=limit * 2**20),
        cost_estimate=pl.CostEstimate(flops=flops, bytes_accessed=2**20, transcendentals=0),
        name=name,
    )(*args)


def on_device(hidden_in, modulation, w_qkv, w_out, qk_gain, stale_kv, positions, order):
    section = lax.axis_index("pipe")
    info = jnp.concatenate([jnp.stack([section]).astype(jnp.int32), order])
    x = hidden_in.reshape(PATCHES, PD, D)
    modulation = jnp.transpose(modulation, (1, 0, 2))
    stale = stale_kv[0].reshape(PATCHES, PD, 2 * D)
    turns = GROUPS + LAYERS - 1
    recv = kbuf = vbuf = tab = None
    fresh, hidden = [], []
    buf = shape(PATCHES, KEYS, HEAD)
    for turn in range(turns):
        first, last = turn == 0, turn == turns - 1
        if first:
            chunk, raw, tab = call(
                functools.partial(project_kernel, turn, last),
                "project0",
                [
                    shape(CHIPS, ROWS + 3 * 2 * PD, HEAD),
                    shape(N, 2 * D),
                    shape(PATCHES, PD, 3 * HEAD, dtype=F32),
                ],
                [info, x, modulation, w_qkv, qk_gain, positions.T, stale],
                40,
                [SMEM, VMEM, VMEM, HBM, VMEM, VMEM, VMEM],
                [pltpu.VMEM((D, 3 * D), BF16), pltpu.SemaphoreType.DMA((9,))],
            )
        else:
            chunk, raw = call(
                functools.partial(project_kernel, turn, last),
                f"project{turn}",
                [
                    shape(CHIPS, ROWS, HEAD),
                    shape(PER, PD, 2, D) if last else shape(N, 2 * D),
                ],
                [info, x, recv, modulation, w_qkv, qk_gain, tab],
            )
        own = lax.all_to_all(chunk, ("z", "x"), 0, 0, tiled=True)
        oth = lax.ppermute(own, "core", [(0, 1), (1, 0)])
        (sums,) = call(
            functools.partial(early_kernel, turn),
            f"early{turn}",
            [shape(PER * QUERIES, 2 * HEAD, dtype=F32)],
            [info, own] + ([] if first else [kbuf, vbuf]),
            flops=3 * 10**9,
        )
        (att,) = call(
            functools.partial(late_kernel, turn),
            f"late{turn}",
            [shape(CHIPS, N, HEAD)],
            [own, oth, sums],
            specs=[VMEM] * 3,
        )
        back = lax.all_to_all(att, ("z", "x"), 0, 0, tiled=True)
        args = [info, back, w_out, x] + ([] if first else [recv]) + [modulation]
        new, *kept = call(
            functools.partial(output_kernel, turn, last),
            f"output{turn}",
            [shape(PATCHES, PD, D), shape(PATCHES, PD, 2, D)] if last else [shape(PER, PD, D)],
            args + (fresh + [raw] + hidden if last else []),
            scratch=[pltpu.VMEM((PER, PD, D), BF16)] + [pltpu.SemaphoreType.DMA((PATCHES,))] * 2
            if last
            else (),
            outs=HBM if last else None,
        )
        hidden.append(new)
        if not last:
            kbuf, vbuf, pair = call(
                functools.partial(keep_kernel, turn),
                f"keep{turn}",
                [buf, buf, shape(PER, PD, 2, D)],
                [info, raw, own, oth] + ([] if first else [kbuf, vbuf]),
            )
            fresh.append(pair)
            recv = lax.ppermute(new, "pipe", [(i, i + 1) for i in range(LAYERS - 1)])
            recv, kbuf, vbuf = lax.optimization_barrier((recv, kbuf, vbuf))
    return (
        hidden[-1].reshape(1, PATCHES * PD, D),
        kept[0].reshape(1, PATCHES * PD, 2, D),
    )


def solution(mesh):
    fine = Mesh(mesh.devices.reshape(4, 4, 4, 2), ("pipe", "z", "x", "core"))
    seq = ("z", "x", "core")
    in_specs = (
        P(seq, None),
        P("pipe", None, None),
        P("pipe", None, None),
        P("pipe", None, None),
        P("pipe", None, None),
        P("pipe", seq, None, None),
        P(seq, None),
        P(),
    )
    out_specs = (P("pipe", seq, None), P("pipe", seq, None, None))
    return jax.shard_map(
        on_device, mesh=fine, in_specs=in_specs, out_specs=out_specs, check_vma=False
    )
```

profile of v0, /device:TPU:24, one launch (start us, length us, event | category | flops | bytes accessed | tf_op | source)
XLA Modules:
  0.0 223.4 jit_solution(15911541765679930650)
XLA Ops:
  3.0 7.5 %project0.1 = (bf16[16,288,128]{2,1,0:T(8,128)(2,1)S(1)}, bf16[48,3072]{1,0:T(8,128)(2,1)S(1)}, f32[4,24,384]{2,1,0:T(8,128)S(1)}) custom-call(s32[5]{0:T(128)S(1)} %pad_add_fusion.refs_0_.info_ref, bf16[4,24,1536]{2,1,0:T(8,128)(2,1)S(1)} %bitcast.10, f32[3,1,1536]{2,1,0:T(1,128)S(1)} %bitcast.20, bf16[1,1536,4608]{2,1,0:T(8,128)(2,1)} %refs_4_.9, ...), custom_call_target="tpu_custom_call" | custom-call | flops 1000000000 | bytes 1048576 | tf_op jit(solution)/shard_map/project0/pallas_call | solution.py:367
  10.6 26.5 %all_to_all.50.own_ref = bf16[16,288,128]{2,1,0:T(8,128)(2,1)S(1)} all-to-all(bf16[16,288,128]{2,1,0:T(8,128)(2,1)S(1)} %get-tuple-element.39), channel_id=1, replica_groups=mesh['pipe'=4,'z'=4,'x'=4,'core'=2] {'z','x'}, dimensions={0} | all-to-all | bytes 2359296 | tf_op jit(solution)/shard_map/all_to_all | solution.py:415
  37.1 2.7 %early0.1.sum_ref = f32[768,256]{1,0:T(8,128)S(1)} custom-call(s32[5]{0:T(128)S(1)} %pad_add_fusion.refs_0_.info_ref, bf16[16,288,128]{2,1,0:T(8,128)(2,1)S(1)} %all_to_all.50.own_ref), custom_call_target="tpu_custom_call" | custom-call | flops 3000000000 | bytes 1048576 | tf_op jit(solution)/shard_map/early0/pallas_call | solution.py:367
  42.2 11.6 %all_to_all.51.refs_1_ = bf16[16,48,128]{2,1,0:T(8,128)(2,1)S(1)} all-to-all(bf16[16,48,128]{2,1,0:T(8,128)(2,1)S(1)} %late0.1), channel_id=1, replica_groups=mesh['pipe'=4,'z'=4,'x'=4,'core'=2] {'z','x'}, dimensions={0} | all-to-all | bytes 393216 | tf_op jit(solution)/shard_map/all_to_all | solution.py:431
  58.0 4.4 %collective-permute-done.1.refs_2_.refs_4_ = bf16[2,24,1536]{2,1,0:T(8,128)(2,1)S(1)} collective-permute-done((bf16[2,24,1536]{2,1,0:T(8,128)(2,1)S(1)}, bf16[2,24,1536]{2,1,0:T(8,128)(2,1)S(1)}, u32[]{:S(2)}, u32[]{:S(2)}) %collective-permute-start.1) | collective-permute-done | bytes 147488 | tf_op jit(solution)/shard_map/ppermute | solution.py:452
  62.4 3.6 %project1.1 = (bf16[16,144,128]{2,1,0:T(8,128)(2,1)S(1)}, bf16[48,3072]{1,0:T(8,128)(2,1)S(1)}) custom-call(s32[5]{0:T(128)S(1)} %pad_add_fusion.refs_0_.info_ref, bf16[4,24,1536]{2,1,0:T(8,128)(2,1)S(1)} %bitcast.12, bf16[2,24,1536]{2,1,0:T(8,128)(2,1)S(1)} %collective-permute-done.1.refs_2_.refs_4_, f32[3,1,1536]{2,1,0:T(1,128)S(1)} %bitcast.22, ...), custom_call_target="tpu_custom_call" | custom-call | flops 1000000000 | bytes 1048576 | tf_op jit(solution)/shard_map/project1/pallas_call | solution.py:367
  66.0 13.5 %all_to_all.52.own_ref = bf16[16,144,128]{2,1,0:T(8,128)(2,1)S(1)} all-to-all(bf16[16,144,128]{2,1,0:T(8,128)(2,1)S(1)} %get-tuple-element.45), channel_id=1, replica_groups=mesh['pipe'=4,'z'=4,'x'=4,'core'=2] {'z','x'}, dimensions={0} | all-to-all | bytes 1179648 | tf_op jit(solution)/shard_map/all_to_all | solution.py:415
  79.6 3.3 %early1.1.sum_ref = f32[768,256]{1,0:T(8,128)S(1)} custom-call(s32[5]{0:T(128)S(1)} %pad_add_fusion.refs_0_.info_ref, bf16[16,144,128]{2,1,0:T(8,128)(2,1)S(1)} %all_to_all.52.own_ref, bf16[4,768,128]{2,1,0:T(8,128)(2,1)S(1)} %get-tuple-element.46.refs_0_, bf16[4,768,128]{2,1,0:T(8,128)(2,1)S(1)} %get-tuple-element.47.refs_1_), custom_call_target="tpu_custom_call" | custom-call | flops 3000000000 | bytes 1048576 | tf_op jit(solution)/shard_map/early1/pallas_call | solution.py:367
  83.7 11.8 %all_to_all.53.refs_1_ = bf16[16,48,128]{2,1,0:T(8,128)(2,1)S(1)} all-to-all(bf16[16,48,128]{2,1,0:T(8,128)(2,1)S(1)} %late1.1), channel_id=1, replica_groups=mesh['pipe'=4,'z'=4,'x'=4,'core'=2] {'z','x'}, dimensions={0} | all-to-all | bytes 393216 | tf_op jit(solution)/shard_map/all_to_all | solution.py:431
  99.4 4.6 %collective-permute-done.3.refs_2_.refs_4_ = bf16[2,24,1536]{2,1,0:T(8,128)(2,1)S(1)} collective-permute-done((bf16[2,24,1536]{2,1,0:T(8,128)(2,1)S(1)}, bf16[2,24,1536]{2,1,0:T(8,128)(2,1)S(1)}, u32[]{:S(2)}, u32[]{:S(2)}) %collective-permute-start.3) | collective-permute-done | bytes 147488 | tf_op jit(solution)/shard_map/ppermute | solution.py:452
  104.0 3.6 %project2.1 = (bf16[16,144,128]{2,1,0:T(8,128)(2,1)S(1)}, bf16[48,3072]{1,0:T(8,128)(2,1)S(1)}) custom-call(s32[5]{0:T(128)S(1)} %pad_add_fusion.refs_0_.info_ref, bf16[4,24,1536]{2,1,0:T(8,128)(2,1)S(1)} %bitcast.14, bf16[2,24,1536]{2,1,0:T(8,128)(2,1)S(1)} %collective-permute-done.3.refs_2_.refs_4_, f32[3,1,1536]{2,1,0:T(1,128)S(1)} %bitcast.24, ...), custom_call_target="tpu_custom_call" | custom-call | flops 1000000000 | bytes 1048576 | tf_op jit(solution)/shard_map/project2/pallas_call | solution.py:367
  107.7 13.6 %all_to_all.54.own_ref = bf16[16,144,128]{2,1,0:T(8,128)(2,1)S(1)} all-to-all(bf16[16,144,128]{2,1,0:T(8,128)(2,1)S(1)} %get-tuple-element.52), channel_id=1, replica_groups=mesh['pipe'=4,'z'=4,'x'=4,'core'=2] {'z','x'}, dimensions={0} | all-to-all | bytes 1179648 | tf_op jit(solution)/shard_map/all_to_all | solution.py:415
  121.2 3.3 %early2.1.sum_ref = f32[768,256]{1,0:T(8,128)S(1)} custom-call(s32[5]{0:T(128)S(1)} %pad_add_fusion.refs_0_.info_ref, bf16[16,144,128]{2,1,0:T(8,128)(2,1)S(1)} %all_to_all.54.own_ref, bf16[4,768,128]{2,1,0:T(8,128)(2,1)S(1)} %get-tuple-element.53.refs_0_, bf16[4,768,128]{2,1,0:T(8,128)(2,1)S(1)} %get-tuple-element.54.refs_1_), custom_call_target="tpu_custom_call" | custom-call | flops 3000000000 | bytes 1048576 | tf_op jit(solution)/shard_map/early2/pallas_call | solution.py:367
  125.4 11.8 %all_to_all.55.refs_1_ = bf16[16,48,128]{2,1,0:T(8,128)(2,1)S(1)} all-to-all(bf16[16,48,128]{2,1,0:T(8,128)(2,1)S(1)} %late2.1), channel_id=1, replica_groups=mesh['pipe'=4,'z'=4,'x'=4,'core'=2] {'z','x'}, dimensions={0} | all-to-all | bytes 393216 | tf_op jit(solution)/shard_map/all_to_all | solution.py:431
  141.1 4.6 %collective-permute-done.5.refs_2_.refs_4_ = bf16[2,24,1536]{2,1,0:T(8,128)(2,1)S(1)} collective-permute-done((bf16[2,24,1536]{2,1,0:T(8,128)(2,1)S(1)}, bf16[2,24,1536]{2,1,0:T(8,128)(2,1)S(1)}, u32[]{:S(2)}, u32[]{:S(2)}) %collective-permute-start.5) | collective-permute-done | bytes 147488 | tf_op jit(solution)/shard_map/ppermute | solution.py:452
  145.7 3.6 %project3.1 = (bf16[16,144,128]{2,1,0:T(8,128)(2,1)S(1)}, bf16[48,3072]{1,0:T(8,128)(2,1)S(1)}) custom-call(s32[5]{0:T(128)S(1)} %pad_add_fusion.refs_0_.info_ref, bf16[4,24,1536]{2,1,0:T(8,128)(2,1)S(1)} %bitcast.16, bf16[2,24,1536]{2,1,0:T(8,128)(2,1)S(1)} %collective-permute-done.5.refs_2_.refs_4_, f32[3,1,1536]{2,1,0:T(1,128)S(1)} %bitcast.26, ...), custom_call_target="tpu_custom_call" | custom-call | flops 1000000000 | bytes 1048576 | tf_op jit(solution)/shard_map/project3/pallas_call | solution.py:367
  149.3 13.6 %all_to_all.56.own_ref = bf16[16,144,128]{2,1,0:T(8,128)(2,1)S(1)} all-to-all(bf16[16,144,128]{2,1,0:T(8,128)(2,1)S(1)} %get-tuple-element.59), channel_id=1, replica_groups=mesh['pipe'=4,'z'=4,'x'=4,'core'=2] {'z','x'}, dimensions={0} | all-to-all | bytes 1179648 | tf_op jit(solution)/shard_map/all_to_all | solution.py:415
  162.9 3.3 %early3.1.sum_ref = f32[768,256]{1,0:T(8,128)S(1)} custom-call(s32[5]{0:T(128)S(1)} %pad_add_fusion.refs_0_.info_ref, bf16[16,144,128]{2,1,0:T(8,128)(2,1)S(1)} %all_to_all.56.own_ref, bf16[4,768,128]{2,1,0:T(8,128)(2,1)S(1)} %get-tuple-element.60.refs_0_, bf16[4,768,128]{2,1,0:T(8,128)(2,1)S(1)} %get-tuple-element.61.refs_1_), custom_call_target="tpu_custom_call" | custom-call | flops 3000000000 | bytes 1048576 | tf_op jit(solution)/shard_map/early3/pallas_call | solution.py:367
  167.1 11.8 %all_to_all.57.refs_1_ = bf16[16,48,128]{2,1,0:T(8,128)(2,1)S(1)} all-to-all(bf16[16,48,128]{2,1,0:T(8,128)(2,1)S(1)} %late3.1), channel_id=1, replica_groups=mesh['pipe'=4,'z'=4,'x'=4,'core'=2] {'z','x'}, dimensions={0} | all-to-all | bytes 393216 | tf_op jit(solution)/shard_map/all_to_all | solution.py:431
  182.8 4.6 %collective-permute-done.7.refs_2_.refs_4_ = bf16[2,24,1536]{2,1,0:T(8,128)(2,1)S(1)} collective-permute-done((bf16[2,24,1536]{2,1,0:T(8,128)(2,1)S(1)}, bf16[2,24,1536]{2,1,0:T(8,128)(2,1)S(1)}, u32[]{:S(2)}, u32[]{:S(2)}) %collective-permute-start.7) | collective-permute-done | bytes 147488 | tf_op jit(solution)/shard_map/ppermute | solution.py:452
  187.4 4.0 %project4.1 = (bf16[16,144,128]{2,1,0:T(8,128)(2,1)S(1)}, bf16[2,24,2,1536]{3,2,1,0:T(2,128)(2,1)S(1)}) custom-call(s32[5]{0:T(128)S(1)} %pad_add_fusion.refs_0_.info_ref, bf16[4,24,1536]{2,1,0:T(8,128)(2,1)S(1)} %bitcast.18, bf16[2,24,1536]{2,1,0:T(8,128)(2,1)S(1)} %collective-permute-done.7.refs_2_.refs_4_, f32[3,1,1536]{2,1,0:T(1,128)S(1)} %bitcast.28, ...), custom_call_target="tpu_custom_call" | custom-call | flops 1000000000 | bytes 1048576 | tf_op jit(solution)/shard_map/project4/pallas_call | solution.py:367
  191.4 13.6 %all_to_all.58.own_ref = bf16[16,144,128]{2,1,0:T(8,128)(2,1)S(1)} all-to-all(bf16[16,144,128]{2,1,0:T(8,128)(2,1)S(1)} %get-tuple-element.66), channel_id=1, replica_groups=mesh['pipe'=4,'z'=4,'x'=4,'core'=2] {'z','x'}, dimensions={0} | all-to-all | bytes 1179648 | tf_op jit(solution)/shard_map/all_to_all | solution.py:415
  205.0 3.3 %early4.1.sum_ref = f32[768,256]{1,0:T(8,128)S(1)} custom-call(s32[5]{0:T(128)S(1)} %pad_add_fusion.refs_0_.info_ref, bf16[16,144,128]{2,1,0:T(8,128)(2,1)S(1)} %all_to_all.58.own_ref, bf16[4,768,128]{2,1,0:T(8,128)(2,1)S(1)} %get-tuple-element.67.refs_0_, bf16[4,768,128]{2,1,0:T(8,128)(2,1)S(1)} %get-tuple-element.68.refs_1_), custom_call_target="tpu_custom_call" | custom-call | flops 3000000000 | bytes 1048576 | tf_op jit(solution)/shard_map/early4/pallas_call | solution.py:367
  209.2 11.8 %all_to_all.59.refs_1_ = bf16[16,48,128]{2,1,0:T(8,128)(2,1)S(1)} all-to-all(bf16[16,48,128]{2,1,0:T(8,128)(2,1)S(1)} %late4.1), channel_id=1, replica_groups=mesh['pipe'=4,'z'=4,'x'=4,'core'=2] {'z','x'}, dimensions={0} | all-to-all | bytes 393216 | tf_op jit(solution)/shard_map/all_to_all | solution.py:431
  (54 shorter events, 26.3 us)
Async XLA Ops:
  0.6 2.3 %copy-start.4 = (s32[4]{0:T(128)S(1)}, s32[4]{0:T(128)}, u32[]{:S(2)}) copy-start(s32[4]{0:T(128)} %param.15) | copy-start | bytes 52
  0.6 2.4 %copy-start = (bf16[96,1536]{1,0:T(8,128)(2,1)S(1)}, bf16[96,1536]{1,0:T(8,128)(2,1)}, u32[]{:S(2)}) copy-start(bf16[96,1536]{1,0:T(8,128)(2,1)} %param.8) | copy-start | bytes 884740
  0.7 2.4 %copy-start.1 = (f32[1,3,1536]{2,0,1:T(1,128)S(1)}, f32[1,3,1536]{2,0,1:T(1,128)}, u32[]{:S(2)}) copy-start(f32[1,3,1536]{2,0,1:T(1,128)} %param.9) | copy-start | bytes 55300
  0.7 2.4 %copy-start.2 = (f32[1,2,128]{2,1,0:T(2,128)S(1)}, f32[1,2,128]{2,1,0:T(2,128)}, u32[]{:S(2)}) copy-start(f32[1,2,128]{2,1,0:T(2,128)} %refs_5_.7) | copy-start | bytes 3076
  0.7 2.3 %copy-start.3 = (s32[96,3]{0,1:T(4,128)S(1)}, s32[96,3]{0,1:T(4,128)}, u32[]{:S(2)}) copy-start(s32[96,3]{0,1:T(4,128)} %param.14) | copy-start | bytes 3460
  3.0 50.8 %slice-start.4 = ((s8[4718592]{0:T(1024)(128)(4,1)}), s8[4194304]{0:T(1024)(128)(4,1)S(1)}, s32[]{:S(2)}) async-start(s8[4718592]{0:T(1024)(128)(4,1)} %bitcast.8), calls=%async_computation.14 | async-start | bytes 8388608
  10.5 43.3 %slice-start.5 = ((s8[4718592]{0:T(1024)(128)(4,1)}), s8[524288]{0:T(1024)(128)(4,1)S(1)}, s32[]{:S(2)}) async-start(s8[4718592]{0:T(1024)(128)(4,1)} %bitcast.8), calls=%async_computation.15 | async-start | bytes 1048576
  10.5 51.9 %slice-start = ((s8[14155776]{0:T(1024)(128)(4,1)}), s8[4194304]{0:T(1024)(128)(4,1)S(1)}, s32[]{:S(2)}) async-start(s8[14155776]{0:T(1024)(128)(4,1)} %bitcast.6), calls=%async_computation.10 | async-start | bytes 8388608
  37.0 25.3 %slice-start.1 = ((s8[14155776]{0:T(1024)(128)(4,1)}), s8[4194304]{0:T(1024)(128)(4,1)S(1)}, s32[]{:S(2)}) async-start(s8[14155776]{0:T(1024)(128)(4,1)} %bitcast.6), calls=%async_computation.11 | async-start | bytes 8388608
  37.0 25.3 %slice-start.2 = ((s8[14155776]{0:T(1024)(128)(4,1)}), s8[4194304]{0:T(1024)(128)(4,1)S(1)}, s32[]{:S(2)}) async-start(s8[14155776]{0:T(1024)(128)(4,1)} %bitcast.6), calls=%async_computation.12 | async-start | bytes 8388608
  37.1 2.8 %collective-permute-start = (bf16[16,288,128]{2,1,0:T(8,128)(2,1)S(1)}, bf16[16,288,128]{2,1,0:T(8,128)(2,1)S(1)}, u32[]{:S(2)}, u32[]{:S(2)}) collective-permute-start(bf16[16,288,128]{2,1,0:T(8,128)(2,1)S(1)} %all_to_all.50.own_ref), channel_id=1, source_target_pairs={{0,1},{1,0},{2,3},{3,2},{4,5},{5,4},{6,7},{7,6},{8,9},{9,8},{10,11... | collective-permute-start | bytes 3538952 | tf_op jit(solution)/shard_map/ppermute | solution.py:416
  53.9 8.5 %slice-start.3 = ((s8[14155776]{0:T(1024)(128)(4,1)}), s8[1572864]{0:T(1024)(128)(4,1)S(1)}, s32[]{:S(2)}) async-start(s8[14155776]{0:T(1024)(128)(4,1)} %bitcast.6), calls=%async_computation.13 | async-start | bytes 3145728
  55.4 7.0 %collective-permute-start.1 = (bf16[2,24,1536]{2,1,0:T(8,128)(2,1)S(1)}, bf16[2,24,1536]{2,1,0:T(8,128)(2,1)S(1)}, u32[]{:S(2)}, u32[]{:S(2)}) collective-permute-start(bf16[2,24,1536]{2,1,0:T(8,128)(2,1)S(1)} %output0.1.refs_11_), channel_id=1, source_target_pairs={{0,32},{32,64},{64,96},{1,33},{33,65},{65,97},{2,34},{34,66},{66,9... | collective-permute-start | bytes 442376 | tf_op jit(solution)/shard_map/ppermute | solution.py:452
  79.5 3.3 %collective-permute-start.2 = (bf16[16,144,128]{2,1,0:T(8,128)(2,1)S(1)}, bf16[16,144,128]{2,1,0:T(8,128)(2,1)S(1)}, u32[]{:S(2)}, u32[]{:S(2)}) collective-permute-start(bf16[16,144,128]{2,1,0:T(8,128)(2,1)S(1)} %all_to_all.52.own_ref), channel_id=1, source_target_pairs={{0,1},{1,0},{2,3},{3,2},{4,5},{5,4},{6,7},{7,6},{8,9},{9,8},{10,11... | collective-permute-start | bytes 1769480 | tf_op jit(solution)/shard_map/ppermute | solution.py:416
  97.0 7.0 %collective-permute-start.3 = (bf16[2,24,1536]{2,1,0:T(8,128)(2,1)S(1)}, bf16[2,24,1536]{2,1,0:T(8,128)(2,1)S(1)}, u32[]{:S(2)}, u32[]{:S(2)}) collective-permute-start(bf16[2,24,1536]{2,1,0:T(8,128)(2,1)S(1)} %output1.1.refs_12_), channel_id=1, source_target_pairs={{0,32},{32,64},{64,96},{1,33},{33,65},{65,97},{2,34},{34,66},{66,9... | collective-permute-start | bytes 442376 | tf_op jit(solution)/shard_map/ppermute | solution.py:452
  121.2 3.3 %collective-permute-start.4 = (bf16[16,144,128]{2,1,0:T(8,128)(2,1)S(1)}, bf16[16,144,128]{2,1,0:T(8,128)(2,1)S(1)}, u32[]{:S(2)}, u32[]{:S(2)}) collective-permute-start(bf16[16,144,128]{2,1,0:T(8,128)(2,1)S(1)} %all_to_all.54.own_ref), channel_id=1, source_target_pairs={{0,1},{1,0},{2,3},{3,2},{4,5},{5,4},{6,7},{7,6},{8,9},{9,8},{10,11... | collective-permute-start | bytes 1769480 | tf_op jit(solution)/shard_map/ppermute | solution.py:416
  138.7 7.0 %collective-permute-start.5 = (bf16[2,24,1536]{2,1,0:T(8,128)(2,1)S(1)}, bf16[2,24,1536]{2,1,0:T(8,128)(2,1)S(1)}, u32[]{:S(2)}, u32[]{:S(2)}) collective-permute-start(bf16[2,24,1536]{2,1,0:T(8,128)(2,1)S(1)} %output2.1.refs_13_), channel_id=1, source_target_pairs={{0,32},{32,64},{64,96},{1,33},{33,65},{65,97},{2,34},{34,66},{66,9... | collective-permute-start | bytes 442376 | tf_op jit(solution)/shard_map/ppermute | solution.py:452
  162.9 3.3 %collective-permute-start.6 = (bf16[16,144,128]{2,1,0:T(8,128)(2,1)S(1)}, bf16[16,144,128]{2,1,0:T(8,128)(2,1)S(1)}, u32[]{:S(2)}, u32[]{:S(2)}) collective-permute-start(bf16[16,144,128]{2,1,0:T(8,128)(2,1)S(1)} %all_to_all.56.own_ref), channel_id=1, source_target_pairs={{0,1},{1,0},{2,3},{3,2},{4,5},{5,4},{6,7},{7,6},{8,9},{9,8},{10,11... | collective-permute-start | bytes 1769480 | tf_op jit(solution)/shard_map/ppermute | solution.py:416
  180.4 7.0 %collective-permute-start.7 = (bf16[2,24,1536]{2,1,0:T(8,128)(2,1)S(1)}, bf16[2,24,1536]{2,1,0:T(8,128)(2,1)S(1)}, u32[]{:S(2)}, u32[]{:S(2)}) collective-permute-start(bf16[2,24,1536]{2,1,0:T(8,128)(2,1)S(1)} %output3.1.refs_14_), channel_id=1, source_target_pairs={{0,32},{32,64},{64,96},{1,33},{33,65},{65,97},{2,34},{34,66},{66,9... | collective-permute-start | bytes 442376 | tf_op jit(solution)/shard_map/ppermute | solution.py:452
  205.0 3.3 %collective-permute-start.8 = (bf16[16,144,128]{2,1,0:T(8,128)(2,1)S(1)}, bf16[16,144,128]{2,1,0:T(8,128)(2,1)S(1)}, u32[]{:S(2)}, u32[]{:S(2)}) collective-permute-start(bf16[16,144,128]{2,1,0:T(8,128)(2,1)S(1)} %all_to_all.58.own_ref), channel_id=1, source_target_pairs={{0,1},{1,0},{2,3},{3,2},{4,5},{5,4},{6,7},{7,6},{8,9},{9,8},{10,11... | collective-permute-start | bytes 1769480 | tf_op jit(solution)/shard_map/ppermute | solution.py:416
where the time goes:
time: 224 us; the launch traced here: 223 us
  blocking collectives  140 us (62%)
  Pallas kernels  56.9 us (25%)
  waiting for transfers between devices  18.3 us (8%)
  starting transfers between devices  5.18 us (2%)
  local copies, waits for them, and re-layouts  2.28 us (1%)
    all_to_all x5, blocking collectives, on_device(): own = lax.all_to_all(chunk, ('z', 'x'), 0, 0, tiled=True)  80.8 us
    all_to_all x5, blocking collectives, on_device(): back = lax.all_to_all(att, ('z', 'x'), 0, 0, tiled=True)  58.8 us
    pallas_call x24, Pallas kernels, call(): pl.pallas_call(kernel, out_shape=out_shape, in_specs=specs or [SMEM] + [V...  56.9 us
    ppermute x4, waiting for transfers between devices, on_device(): recv = lax.ppermute(new, 'pipe', [(i, i + 1) for i in range(LAYERS - 1)])  18.1 us
    ppermute x4, starting transfers between devices, on_device(): recv = lax.ppermute(new, 'pipe', [(i, i + 1) for i in range(LAYERS - 1)])  5.17 us
  transfers between devices with their start and end apart: 9, of which 5 were waited for; matrix products, arithmetic and copies ran while one was open for 0% of the time, Pallas kernels for 9%

commit v1 on v0

--- a/solution.py
+++ b/solution.py
@@ -108,7 +108,7 @@
                         w_ref.at[0, :, cols], held_ref.at[:, cols], sems.at[len(copies)]
                     )
                 )
-        for copy in copies[:6]:
+        for copy in copies:
             copy.start()
         tab_ref[...] = rotary_tables(pos_ref[...]).reshape(PATCHES, PD, 3 * HEAD)
         tabs = jnp.concatenate([tab_ref[info_ref[1 + r]] for r in range(1, PATCHES)], axis=0)
@@ -147,8 +147,6 @@
     def step(block, carry):
         if first and block == 0:
             stale_block(0)
-            for copy in copies[6:]:
-                copy.start()
         done = []
         for part in range(3):
             cols = lanes_from(part * D + block * WIDE)
@@ -184,7 +182,7 @@
             chunk_ref[h, :ROWS] = jnp.concatenate(parts, axis=0).astype(BF16)
         return carry
 
-    if first:
+    if turn < 2:
         for block in range(D // WIDE):
             step(block, 0)
     else:

time: 224 us -> 224 us (level)
  no operation moved by 1% of the time
where the time goes in v1:
time: 224 us; the launch traced here: 223 us
  blocking collectives  140 us (62%)
  Pallas kernels  56.7 us (25%)
  waiting for transfers between devices  18.1 us (8%)
  starting transfers between devices  5.36 us (2%)
  local copies, waits for them, and re-layouts  2.28 us (1%)
    all_to_all x5, blocking collectives, on_device(): own = lax.all_to_all(chunk, ('z', 'x'), 0, 0, tiled=True)  80.8 us
    all_to_all x5, blocking collectives, on_device(): back = lax.all_to_all(att, ('z', 'x'), 0, 0, tiled=True)  58.8 us
    pallas_call x24, Pallas kernels, call(): pl.pallas_call(kernel, out_shape=out_shape, in_specs=specs or [SMEM] + [V...  56.7 us
    ppermute x4, waiting for transfers between devices, on_device(): recv = lax.ppermute(new, 'pipe', [(i, i + 1) for i in range(LAYERS - 1)])  17.9 us
    ppermute x4, starting transfers between devices, on_device(): recv = lax.ppermute(new, 'pipe', [(i, i + 1) for i in range(LAYERS - 1)])  5.35 us
  transfers between devices with their start and end apart: 9, of which 5 were waited for; matrix products, arithmetic and copies ran while one was open for 0% of the time, Pallas kernels for 9%

profile of v1, /device:TPU:24, one launch (start us, length us, event | category | flops | bytes accessed | tf_op | source)
XLA Modules:
  0.0 223.2 jit_solution(3633760143886110684)
XLA Ops:
  3.0 7.5 %project0.1 = (bf16[16,288,128]{2,1,0:T(8,128)(2,1)S(1)}, bf16[48,3072]{1,0:T(8,128)(2,1)S(1)}, f32[4,24,384]{2,1,0:T(8,128)S(1)}) custom-call(s32[5]{0:T(128)S(1)} %pad_add_fusion.refs_0_.info_ref, bf16[4,24,1536]{2,1,0:T(8,128)(2,1)S(1)} %bitcast.10, f32[3,1,1536]{2,1,0:T(1,128)S(1)} %bitcast.20, bf16[1,1536,4608]{2,1,0:T(8,128)(2,1)} %refs_4_.9, ...), custom_call_target="tpu_custom_call" | custom-call | flops 1000000000 | bytes 1048576 | tf_op jit(solution)/shard_map/project0/pallas_call | solution.py:365
  10.6 26.5 %all_to_all.50.own_ref = bf16[16,288,128]{2,1,0:T(8,128)(2,1)S(1)} all-to-all(bf16[16,288,128]{2,1,0:T(8,128)(2,1)S(1)} %get-tuple-element.39), channel_id=1, replica_groups=mesh['pipe'=4,'z'=4,'x'=4,'core'=2] {'z','x'}, dimensions={0} | all-to-all | bytes 2359296 | tf_op jit(solution)/shard_map/all_to_all | solution.py:413
  37.1 2.7 %early0.1.sum_ref = f32[768,256]{1,0:T(8,128)S(1)} custom-call(s32[5]{0:T(128)S(1)} %pad_add_fusion.refs_0_.info_ref, bf16[16,288,128]{2,1,0:T(8,128)(2,1)S(1)} %all_to_all.50.own_ref), custom_call_target="tpu_custom_call" | custom-call | flops 3000000000 | bytes 1048576 | tf_op jit(solution)/shard_map/early0/pallas_call | solution.py:365
  42.2 11.6 %all_to_all.51.refs_1_ = bf16[16,48,128]{2,1,0:T(8,128)(2,1)S(1)} all-to-all(bf16[16,48,128]{2,1,0:T(8,128)(2,1)S(1)} %late0.1), channel_id=1, replica_groups=mesh['pipe'=4,'z'=4,'x'=4,'core'=2] {'z','x'}, dimensions={0} | all-to-all | bytes 393216 | tf_op jit(solution)/shard_map/all_to_all | solution.py:429
  58.2 4.2 %collective-permute-done.1.refs_2_.refs_4_ = bf16[2,24,1536]{2,1,0:T(8,128)(2,1)S(1)} collective-permute-done((bf16[2,24,1536]{2,1,0:T(8,128)(2,1)S(1)}, bf16[2,24,1536]{2,1,0:T(8,128)(2,1)S(1)}, u32[]{:S(2)}, u32[]{:S(2)}) %collective-permute-start.1) | collective-permute-done | bytes 147488 | tf_op jit(solution)/shard_map/ppermute | solution.py:450
  62.4 3.3 %project1.1 = (bf16[16,144,128]{2,1,0:T(8,128)(2,1)S(1)}, bf16[48,3072]{1,0:T(8,128)(2,1)S(1)}) custom-call(s32[5]{0:T(128)S(1)} %pad_add_fusion.refs_0_.info_ref, bf16[4,24,1536]{2,1,0:T(8,128)(2,1)S(1)} %bitcast.12, bf16[2,24,1536]{2,1,0:T(8,128)(2,1)S(1)} %collective-permute-done.1.refs_2_.refs_4_, f32[3,1,1536]{2,1,0:T(1,128)S(1)} %bitcast.22, ...), custom_call_target="tpu_custom_call" | custom-call | flops 1000000000 | bytes 1048576 | tf_op jit(solution)/shard_map/project1/pallas_call | solution.py:365
  65.8 13.5 %all_to_all.52.own_ref = bf16[16,144,128]{2,1,0:T(8,128)(2,1)S(1)} all-to-all(bf16[16,144,128]{2,1,0:T(8,128)(2,1)S(1)} %get-tuple-element.45), channel_id=1, replica_groups=mesh['pipe'=4,'z'=4,'x'=4,'core'=2] {'z','x'}, dimensions={0} | all-to-all | bytes 1179648 | tf_op jit(solution)/shard_map/all_to_all | solution.py:413
  79.3 3.3 %early1.1.sum_ref = f32[768,256]{1,0:T(8,128)S(1)} custom-call(s32[5]{0:T(128)S(1)} %pad_add_fusion.refs_0_.info_ref, bf16[16,144,128]{2,1,0:T(8,128)(2,1)S(1)} %all_to_all.52.own_ref, bf16[4,768,128]{2,1,0:T(8,128)(2,1)S(1)} %get-tuple-element.46.refs_0_, bf16[4,768,128]{2,1,0:T(8,128)(2,1)S(1)} %get-tuple-element.47.refs_1_), custom_call_target="tpu_custom_call" | custom-call | flops 3000000000 | bytes 1048576 | tf_op jit(solution)/shard_map/early1/pallas_call | solution.py:365
  83.4 11.8 %all_to_all.53.refs_1_ = bf16[16,48,128]{2,1,0:T(8,128)(2,1)S(1)} all-to-all(bf16[16,48,128]{2,1,0:T(8,128)(2,1)S(1)} %late1.1), channel_id=1, replica_groups=mesh['pipe'=4,'z'=4,'x'=4,'core'=2] {'z','x'}, dimensions={0} | all-to-all | bytes 393216 | tf_op jit(solution)/shard_map/all_to_all | solution.py:429
  99.2 4.6 %collective-permute-done.3.refs_2_.refs_4_ = bf16[2,24,1536]{2,1,0:T(8,128)(2,1)S(1)} collective-permute-done((bf16[2,24,1536]{2,1,0:T(8,128)(2,1)S(1)}, bf16[2,24,1536]{2,1,0:T(8,128)(2,1)S(1)}, u32[]{:S(2)}, u32[]{:S(2)}) %collective-permute-start.3) | collective-permute-done | bytes 147488 | tf_op jit(solution)/shard_map/ppermute | solution.py:450
  103.7 3.6 %project2.1 = (bf16[16,144,128]{2,1,0:T(8,128)(2,1)S(1)}, bf16[48,3072]{1,0:T(8,128)(2,1)S(1)}) custom-call(s32[5]{0:T(128)S(1)} %pad_add_fusion.refs_0_.info_ref, bf16[4,24,1536]{2,1,0:T(8,128)(2,1)S(1)} %bitcast.14, bf16[2,24,1536]{2,1,0:T(8,128)(2,1)S(1)} %collective-permute-done.3.refs_2_.refs_4_, f32[3,1,1536]{2,1,0:T(1,128)S(1)} %bitcast.24, ...), custom_call_target="tpu_custom_call" | custom-call | flops 1000000000 | bytes 1048576 | tf_op jit(solution)/shard_map/project2/pallas_call | solution.py:365
  107.4 13.6 %all_to_all.54.own_ref = bf16[16,144,128]{2,1,0:T(8,128)(2,1)S(1)} all-to-all(bf16[16,144,128]{2,1,0:T(8,128)(2,1)S(1)} %get-tuple-element.52), channel_id=1, replica_groups=mesh['pipe'=4,'z'=4,'x'=4,'core'=2] {'z','x'}, dimensions={0} | all-to-all | bytes 1179648 | tf_op jit(solution)/shard_map/all_to_all | solution.py:413
  121.0 3.3 %early2.1.sum_ref = f32[768,256]{1,0:T(8,128)S(1)} custom-call(s32[5]{0:T(128)S(1)} %pad_add_fusion.refs_0_.info_ref, bf16[16,144,128]{2,1,0:T(8,128)(2,1)S(1)} %all_to_all.54.own_ref, bf16[4,768,128]{2,1,0:T(8,128)(2,1)S(1)} %get-tuple-element.53.refs_0_, bf16[4,768,128]{2,1,0:T(8,128)(2,1)S(1)} %get-tuple-element.54.refs_1_), custom_call_target="tpu_custom_call" | custom-call | flops 3000000000 | bytes 1048576 | tf_op jit(solution)/shard_map/early2/pallas_call | solution.py:365
  125.1 11.8 %all_to_all.55.refs_1_ = bf16[16,48,128]{2,1,0:T(8,128)(2,1)S(1)} all-to-all(bf16[16,48,128]{2,1,0:T(8,128)(2,1)S(1)} %late2.1), channel_id=1, replica_groups=mesh['pipe'=4,'z'=4,'x'=4,'core'=2] {'z','x'}, dimensions={0} | all-to-all | bytes 393216 | tf_op jit(solution)/shard_map/all_to_all | solution.py:429
  140.9 4.6 %collective-permute-done.5.refs_2_.refs_4_ = bf16[2,24,1536]{2,1,0:T(8,128)(2,1)S(1)} collective-permute-done((bf16[2,24,1536]{2,1,0:T(8,128)(2,1)S(1)}, bf16[2,24,1536]{2,1,0:T(8,128)(2,1)S(1)}, u32[]{:S(2)}, u32[]{:S(2)}) %collective-permute-start.5) | collective-permute-done | bytes 147488 | tf_op jit(solution)/shard_map/ppermute | solution.py:450
  145.4 3.6 %project3.1 = (bf16[16,144,128]{2,1,0:T(8,128)(2,1)S(1)}, bf16[48,3072]{1,0:T(8,128)(2,1)S(1)}) custom-call(s32[5]{0:T(128)S(1)} %pad_add_fusion.refs_0_.info_ref, bf16[4,24,1536]{2,1,0:T(8,128)(2,1)S(1)} %bitcast.16, bf16[2,24,1536]{2,1,0:T(8,128)(2,1)S(1)} %collective-permute-done.5.refs_2_.refs_4_, f32[3,1,1536]{2,1,0:T(1,128)S(1)} %bitcast.26, ...), custom_call_target="tpu_custom_call" | custom-call | flops 1000000000 | bytes 1048576 | tf_op jit(solution)/shard_map/project3/pallas_call | solution.py:365
  149.1 13.6 %all_to_all.56.own_ref = bf16[16,144,128]{2,1,0:T(8,128)(2,1)S(1)} all-to-all(bf16[16,144,128]{2,1,0:T(8,128)(2,1)S(1)} %get-tuple-element.59), channel_id=1, replica_groups=mesh['pipe'=4,'z'=4,'x'=4,'core'=2] {'z','x'}, dimensions={0} | all-to-all | bytes 1179648 | tf_op jit(solution)/shard_map/all_to_all | solution.py:413
  162.7 3.3 %early3.1.sum_ref = f32[768,256]{1,0:T(8,128)S(1)} custom-call(s32[5]{0:T(128)S(1)} %pad_add_fusion.refs_0_.info_ref, bf16[16,144,128]{2,1,0:T(8,128)(2,1)S(1)} %all_to_all.56.own_ref, bf16[4,768,128]{2,1,0:T(8,128)(2,1)S(1)} %get-tuple-element.60.refs_0_, bf16[4,768,128]{2,1,0:T(8,128)(2,1)S(1)} %get-tuple-element.61.refs_1_), custom_call_target="tpu_custom_call" | custom-call | flops 3000000000 | bytes 1048576 | tf_op jit(solution)/shard_map/early3/pallas_call | solution.py:365
  166.8 11.8 %all_to_all.57.refs_1_ = bf16[16,48,128]{2,1,0:T(8,128)(2,1)S(1)} all-to-all(bf16[16,48,128]{2,1,0:T(8,128)(2,1)S(1)} %late3.1), channel_id=1, replica_groups=mesh['pipe'=4,'z'=4,'x'=4,'core'=2] {'z','x'}, dimensions={0} | all-to-all | bytes 393216 | tf_op jit(solution)/shard_map/all_to_all | solution.py:429
  182.6 4.6 %collective-permute-done.7.refs_2_.refs_4_ = bf16[2,24,1536]{2,1,0:T(8,128)(2,1)S(1)} collective-permute-done((bf16[2,24,1536]{2,1,0:T(8,128)(2,1)S(1)}, bf16[2,24,1536]{2,1,0:T(8,128)(2,1)S(1)}, u32[]{:S(2)}, u32[]{:S(2)}) %collective-permute-start.7) | collective-permute-done | bytes 147488 | tf_op jit(solution)/shard_map/ppermute | solution.py:450
  187.1 4.0 %project4.1 = (bf16[16,144,128]{2,1,0:T(8,128)(2,1)S(1)}, bf16[2,24,2,1536]{3,2,1,0:T(2,128)(2,1)S(1)}) custom-call(s32[5]{0:T(128)S(1)} %pad_add_fusion.refs_0_.info_ref, bf16[4,24,1536]{2,1,0:T(8,128)(2,1)S(1)} %bitcast.18, bf16[2,24,1536]{2,1,0:T(8,128)(2,1)S(1)} %collective-permute-done.7.refs_2_.refs_4_, f32[3,1,1536]{2,1,0:T(1,128)S(1)} %bitcast.28, ...), custom_call_target="tpu_custom_call" | custom-call | flops 1000000000 | bytes 1048576 | tf_op jit(solution)/shard_map/project4/pallas_call | solution.py:365
  191.2 13.6 %all_to_all.58.own_ref = bf16[16,144,128]{2,1,0:T(8,128)(2,1)S(1)} all-to-all(bf16[16,144,128]{2,1,0:T(8,128)(2,1)S(1)} %get-tuple-element.66), channel_id=1, replica_groups=mesh['pipe'=4,'z'=4,'x'=4,'core'=2] {'z','x'}, dimensions={0} | all-to-all | bytes 1179648 | tf_op jit(solution)/shard_map/all_to_all | solution.py:413
  204.8 3.3 %early4.1.sum_ref = f32[768,256]{1,0:T(8,128)S(1)} custom-call(s32[5]{0:T(128)S(1)} %pad_add_fusion.refs_0_.info_ref, bf16[16,144,128]{2,1,0:T(8,128)(2,1)S(1)} %all_to_all.58.own_ref, bf16[4,768,128]{2,1,0:T(8,128)(2,1)S(1)} %get-tuple-element.67.refs_0_, bf16[4,768,128]{2,1,0:T(8,128)(2,1)S(1)} %get-tuple-element.68.refs_1_), custom_call_target="tpu_custom_call" | custom-call | flops 3000000000 | bytes 1048576 | tf_op jit(solution)/shard_map/early4/pallas_call | solution.py:365
  208.9 11.8 %all_to_all.59.refs_1_ = bf16[16,48,128]{2,1,0:T(8,128)(2,1)S(1)} all-to-all(bf16[16,48,128]{2,1,0:T(8,128)(2,1)S(1)} %late4.1), channel_id=1, replica_groups=mesh['pipe'=4,'z'=4,'x'=4,'core'=2] {'z','x'}, dimensions={0} | all-to-all | bytes 393216 | tf_op jit(solution)/shard_map/all_to_all | solution.py:429
  (54 shorter events, 26.5 us)
Async XLA Ops:
  0.6 2.3 %copy-start.4 = (s32[4]{0:T(128)S(1)}, s32[4]{0:T(128)}, u32[]{:S(2)}) copy-start(s32[4]{0:T(128)} %param.15) | copy-start | bytes 52
  0.6 2.4 %copy-start = (bf16[96,1536]{1,0:T(8,128)(2,1)S(1)}, bf16[96,1536]{1,0:T(8,128)(2,1)}, u32[]{:S(2)}) copy-start(bf16[96,1536]{1,0:T(8,128)(2,1)} %param.8) | copy-start | bytes 884740
  0.7 2.4 %copy-start.1 = (f32[1,3,1536]{2,0,1:T(1,128)S(1)}, f32[1,3,1536]{2,0,1:T(1,128)}, u32[]{:S(2)}) copy-start(f32[1,3,1536]{2,0,1:T(1,128)} %param.9) | copy-start | bytes 55300
  0.7 2.4 %copy-start.2 = (f32[1,2,128]{2,1,0:T(2,128)S(1)}, f32[1,2,128]{2,1,0:T(2,128)}, u32[]{:S(2)}) copy-start(f32[1,2,128]{2,1,0:T(2,128)} %refs_5_.7) | copy-start | bytes 3076
  0.7 2.3 %copy-start.3 = (s32[96,3]{0,1:T(4,128)S(1)}, s32[96,3]{0,1:T(4,128)}, u32[]{:S(2)}) copy-start(s32[96,3]{0,1:T(4,128)} %param.14) | copy-start | bytes 3460
  3.0 50.8 %slice-start.4 = ((s8[4718592]{0:T(1024)(128)(4,1)}), s8[4194304]{0:T(1024)(128)(4,1)S(1)}, s32[]{:S(2)}) async-start(s8[4718592]{0:T(1024)(128)(4,1)} %bitcast.8), calls=%async_computation.14 | async-start | bytes 8388608
  10.5 43.3 %slice-start.5 = ((s8[4718592]{0:T(1024)(128)(4,1)}), s8[524288]{0:T(1024)(128)(4,1)S(1)}, s32[]{:S(2)}) async-start(s8[4718592]{0:T(1024)(128)(4,1)} %bitcast.8), calls=%async_computation.15 | async-start | bytes 1048576
  10.5 51.9 %slice-start = ((s8[14155776]{0:T(1024)(128)(4,1)}), s8[4194304]{0:T(1024)(128)(4,1)S(1)}, s32[]{:S(2)}) async-start(s8[14155776]{0:T(1024)(128)(4,1)} %bitcast.6), calls=%async_computation.10 | async-start | bytes 8388608
  37.0 25.3 %slice-start.1 = ((s8[14155776]{0:T(1024)(128)(4,1)}), s8[4194304]{0:T(1024)(128)(4,1)S(1)}, s32[]{:S(2)}) async-start(s8[14155776]{0:T(1024)(128)(4,1)} %bitcast.6), calls=%async_computation.11 | async-start | bytes 8388608
  37.0 25.3 %slice-start.2 = ((s8[14155776]{0:T(1024)(128)(4,1)}), s8[4194304]{0:T(1024)(128)(4,1)S(1)}, s32[]{:S(2)}) async-start(s8[14155776]{0:T(1024)(128)(4,1)} %bitcast.6), calls=%async_computation.12 | async-start | bytes 8388608
  37.1 2.8 %collective-permute-start = (bf16[16,288,128]{2,1,0:T(8,128)(2,1)S(1)}, bf16[16,288,128]{2,1,0:T(8,128)(2,1)S(1)}, u32[]{:S(2)}, u32[]{:S(2)}) collective-permute-start(bf16[16,288,128]{2,1,0:T(8,128)(2,1)S(1)} %all_to_all.50.own_ref), channel_id=1, source_target_pairs={{0,1},{1,0},{2,3},{3,2},{4,5},{5,4},{6,7},{7,6},{8,9},{9,8},{10,11... | collective-permute-start | bytes 3538952 | tf_op jit(solution)/shard_map/ppermute | solution.py:414
  53.9 8.5 %slice-start.3 = ((s8[14155776]{0:T(1024)(128)(4,1)}), s8[1572864]{0:T(1024)(128)(4,1)S(1)}, s32[]{:S(2)}) async-start(s8[14155776]{0:T(1024)(128)(4,1)} %bitcast.6), calls=%async_computation.13 | async-start | bytes 3145728
  55.4 7.0 %collective-permute-start.1 = (bf16[2,24,1536]{2,1,0:T(8,128)(2,1)S(1)}, bf16[2,24,1536]{2,1,0:T(8,128)(2,1)S(1)}, u32[]{:S(2)}, u32[]{:S(2)}) collective-permute-start(bf16[2,24,1536]{2,1,0:T(8,128)(2,1)S(1)} %output0.1.refs_11_), channel_id=1, source_target_pairs={{0,32},{32,64},{64,96},{1,33},{33,65},{65,97},{2,34},{34,66},{66,9... | collective-permute-start | bytes 442376 | tf_op jit(solution)/shard_map/ppermute | solution.py:450
  79.3 3.3 %collective-permute-start.2 = (bf16[16,144,128]{2,1,0:T(8,128)(2,1)S(1)}, bf16[16,144,128]{2,1,0:T(8,128)(2,1)S(1)}, u32[]{:S(2)}, u32[]{:S(2)}) collective-permute-start(bf16[16,144,128]{2,1,0:T(8,128)(2,1)S(1)} %all_to_all.52.own_ref), channel_id=1, source_target_pairs={{0,1},{1,0},{2,3},{3,2},{4,5},{5,4},{6,7},{7,6},{8,9},{9,8},{10,11... | collective-permute-start | bytes 1769480 | tf_op jit(solution)/shard_map/ppermute | solution.py:414
  96.7 7.0 %collective-permute-start.3 = (bf16[2,24,1536]{2,1,0:T(8,128)(2,1)S(1)}, bf16[2,24,1536]{2,1,0:T(8,128)(2,1)S(1)}, u32[]{:S(2)}, u32[]{:S(2)}) collective-permute-start(bf16[2,24,1536]{2,1,0:T(8,128)(2,1)S(1)} %output1.1.refs_12_), channel_id=1, source_target_pairs={{0,32},{32,64},{64,96},{1,33},{33,65},{65,97},{2,34},{34,66},{66,9... | collective-permute-start | bytes 442376 | tf_op jit(solution)/shard_map/ppermute | solution.py:450
  121.0 3.3 %collective-permute-start.4 = (bf16[16,144,128]{2,1,0:T(8,128)(2,1)S(1)}, bf16[16,144,128]{2,1,0:T(8,128)(2,1)S(1)}, u32[]{:S(2)}, u32[]{:S(2)}) collective-permute-start(bf16[16,144,128]{2,1,0:T(8,128)(2,1)S(1)} %all_to_all.54.own_ref), channel_id=1, source_target_pairs={{0,1},{1,0},{2,3},{3,2},{4,5},{5,4},{6,7},{7,6},{8,9},{9,8},{10,11... | collective-permute-start | bytes 1769480 | tf_op jit(solution)/shard_map/ppermute | solution.py:414
  138.4 7.0 %collective-permute-start.5 = (bf16[2,24,1536]{2,1,0:T(8,128)(2,1)S(1)}, bf16[2,24,1536]{2,1,0:T(8,128)(2,1)S(1)}, u32[]{:S(2)}, u32[]{:S(2)}) collective-permute-start(bf16[2,24,1536]{2,1,0:T(8,128)(2,1)S(1)} %output2.1.refs_13_), channel_id=1, source_target_pairs={{0,32},{32,64},{64,96},{1,33},{33,65},{65,97},{2,34},{34,66},{66,9... | collective-permute-start | bytes 442376 | tf_op jit(solution)/shard_map/ppermute | solution.py:450
  162.7 3.3 %collective-permute-start.6 = (bf16[16,144,128]{2,1,0:T(8,128)(2,1)S(1)}, bf16[16,144,128]{2,1,0:T(8,128)(2,1)S(1)}, u32[]{:S(2)}, u32[]{:S(2)}) collective-permute-start(bf16[16,144,128]{2,1,0:T(8,128)(2,1)S(1)} %all_to_all.56.own_ref), channel_id=1, source_target_pairs={{0,1},{1,0},{2,3},{3,2},{4,5},{5,4},{6,7},{7,6},{8,9},{9,8},{10,11... | collective-permute-start | bytes 1769480 | tf_op jit(solution)/shard_map/ppermute | solution.py:414
  180.1 7.0 %collective-permute-start.7 = (bf16[2,24,1536]{2,1,0:T(8,128)(2,1)S(1)}, bf16[2,24,1536]{2,1,0:T(8,128)(2,1)S(1)}, u32[]{:S(2)}, u32[]{:S(2)}) collective-permute-start(bf16[2,24,1536]{2,1,0:T(8,128)(2,1)S(1)} %output3.1.refs_14_), channel_id=1, source_target_pairs={{0,32},{32,64},{64,96},{1,33},{33,65},{65,97},{2,34},{34,66},{66,9... | collective-permute-start | bytes 442376 | tf_op jit(solution)/shard_map/ppermute | solution.py:450
  204.8 3.3 %collective-permute-start.8 = (bf16[16,144,128]{2,1,0:T(8,128)(2,1)S(1)}, bf16[16,144,128]{2,1,0:T(8,128)(2,1)S(1)}, u32[]{:S(2)}, u32[]{:S(2)}) collective-permute-start(bf16[16,144,128]{2,1,0:T(8,128)(2,1)S(1)} %all_to_all.58.own_ref), channel_id=1, source_target_pairs={{0,1},{1,0},{2,3},{3,2},{4,5},{5,4},{6,7},{7,6},{8,9},{9,8},{10,11... | collective-permute-start | bytes 1769480 | tf_op jit(solution)/shard_map/ppermute | solution.py:414
